TPU v7x, 32 devices: a whole 2x2x4 slice. The times are simulated.
32 devices in a mesh: groups: 2 (over x), dp: 2 (over core), tensor: 8 (over z, y).
Axes of the slice: x: 2, y: 2, z: 4, core: 2. Of those that a mesh axis runs over, the one named last changes fastest.
Arguments:
- hidden: bfloat16 [1536, 16384], P(('groups', 'dp'), 'tensor'), parts along dimension 0, may hold values from -6 to 6
- down_matrix: bfloat16 [16384, 8192], P('tensor'), may hold values from -0.0625 to 0.0625
- rank_input_map: bfloat16 [32, 16, 16384], P(None, None, 'tensor'), may hold values from -0.046875 to 0.046875
- rank_output_map: bfloat16 [32, 16, 8192], P(None, None, 'tensor'), may hold values from -0.75 to 0.75
- job_row_counts: int32 [64], P('groups'), parts along dimension 0, may hold values from 1 to 192, 768 in all
- output_gradient: bfloat16 [1536, 8192], P(('groups', 'dp'), 'tensor'), parts along dimension 0, may hold values from -6 to 6
Outputs:
- mixed: bfloat16 [1536, 8192], P(('groups', 'dp'), 'tensor'), parts along dimension 0
- grad_hidden: bfloat16 [1536, 16384], P(('groups', 'dp'), 'tensor'), parts along dimension 0
- grad_a: float32 [64, 16, 16384], P(('groups', 'dp'), None, 'tensor'), parts along dimension 0
- grad_b: float32 [64, 16, 8192], P(('groups', 'dp'), None, 'tensor'), parts along dimension 0
There are 2 independent parts, one for each index of `groups`. A program takes and returns all parts, laid end to end along the dimension named above; an argument that names none is the same for every part. Nothing has to cross between parts.
Inputs may be any that keep to these rules, and one draw needn't show every extreme that they name: `job_row_counts`: the counts sum to 768 and the largest is exactly 192.
All inputs are finite; a program needn't handle non-finite values.
Results may differ from a plain program's by a relative error of at most 0.014.
Values may be sent and summed in bfloat16 or wider, within the bound.
A program may use at most 192 MiB of HBM per device.

v0:
```python
import jax
import jax.numpy as jnp
from jax import lax
from jax.sharding import PartitionSpec as P

SCALE = 2.0


def select(spread, member, rank_count):
    job_count = member.shape[0]
    return jnp.sum(
        spread.reshape(job_count, rank_count, member.shape[1]) * member[:, None, :], axis=0
    )


def expand(values, member):
    job_count, rows = member.shape
    full = member[:, None, :] * values.astype(jnp.float32)[None, :, :]
    return full.reshape(job_count * values.shape[0], rows).astype(jnp.bfloat16)


def body(hidden, down_matrix, rank_input_map, rank_output_map, job_row_counts, output_gradient):
    rows_dev, local_hidden = hidden.shape
    job_count, rank_count, local_width = rank_output_map.shape
    input_adapter = rank_input_map.reshape(job_count * rank_count, local_hidden)
    output_adapter = rank_output_map.reshape(job_count * rank_count, local_width)
    positions = lax.axis_index("dp") * rows_dev + lax.iota(jnp.int32, rows_dev)
    ends = jnp.cumsum(job_row_counts)
    starts = ends - job_row_counts
    member = (
        (positions[None, :] >= starts[:, None]) & (positions[None, :] < ends[:, None])
    ).astype(jnp.float32)
    dims = (((1,), (1,)), ((), ()))
    lead = (((0,), (0,)), ((), ()))
    low_part = select(
        lax.dot_general(input_adapter, hidden, dims, preferred_element_type=jnp.float32),
        member,
        rank_count,
    )
    back_part = select(
        lax.dot_general(output_adapter, output_gradient, dims, preferred_element_type=jnp.float32),
        member,
        rank_count,
    )
    low = lax.psum(low_part, "tensor")
    back_low = lax.psum(back_part, "tensor")
    low_wide = expand((SCALE * low).astype(jnp.bfloat16), member)
    back_wide = expand((SCALE * back_low).astype(jnp.bfloat16), member)
    cross = (((0,), (1,)), ((), ()))
    weight_cols = down_matrix
    base = (
        lax.psum_scatter(
            lax.dot_general(weight_cols, hidden, cross, preferred_element_type=jnp.float32).astype(
                jnp.bfloat16
            ),
            "tensor",
            scatter_dimension=0,
            tiled=True,
        )
        .astype(jnp.float32)
        .T
    )
    adapter_out = lax.dot_general(
        low_wide, output_adapter, lead, preferred_element_type=jnp.float32
    )
    mixed = (base + adapter_out).astype(jnp.bfloat16)
    grad_b_local = jnp.dot(low_wide, output_gradient, preferred_element_type=jnp.float32).reshape(
        job_count, rank_count, local_width
    )
    grad_a_local = jnp.dot(back_wide, hidden, preferred_element_type=jnp.float32).reshape(
        job_count, rank_count, local_hidden
    )
    total_a, total_b = (
        lax.psum(grad_a_local.astype(jnp.bfloat16), "dp").astype(jnp.float32),
        lax.psum(grad_b_local.astype(jnp.bfloat16), "dp").astype(jnp.float32),
    )
    share = job_count // lax.axis_size("dp")
    offset = lax.axis_index("dp") * share
    grad_a = lax.dynamic_slice_in_dim(total_a, offset, share, 0)
    grad_b = lax.dynamic_slice_in_dim(total_b, offset, share, 0)
    weight_cols = down_matrix
    through = lax.dot_general(
        lax.all_gather(output_gradient, "tensor", axis=1, tiled=True),
        weight_cols,
        dims,
        preferred_element_type=jnp.float32,
    )
    adapter_back = lax.dot_general(
        back_wide, input_adapter, lead, preferred_element_type=jnp.float32
    )
    grad_hidden = (through + adapter_back).astype(jnp.bfloat16)
    return (mixed, grad_hidden, grad_a, grad_b)


def solution(mesh):
    placed = (
        P(("groups", "dp"), "tensor"),
        P("tensor", None),
        P(None, None, "tensor"),
        P(None, None, "tensor"),
        P("groups"),
        P(("groups", "dp"), "tensor"),
    )
    return jax.shard_map(
        body,
        mesh=mesh,
        in_specs=placed,
        out_specs=(
            P(("groups", "dp"), "tensor"),
            P(("groups", "dp"), "tensor"),
            P(("groups", "dp"), None, "tensor"),
            P(("groups", "dp"), None, "tensor"),
        ),
        check_vma=False,
    )
```

profile of v0, /device:TPU:10, one launch (start us, length us, event | category | flops | bytes accessed | tf_op | source)
XLA Modules:
  0.0 285.2 jit_solution(16441169541885111114)
XLA Ops:
  8.0 0.0 all-reduce.4.cloned.1.call-start
  8.1 0.9 copy.17
  8.9 0.1 reduce-window.8
  9.0 0.1 reduce
  9.1 0.7 sub.3
  9.8 0.1 and_convert_fusion
  9.9 2.8 fusion.8
  12.7 0.7 fusion.11
  13.5 35.1 %all-reduce = (f32[16,384]{1,0:T(8,128)S(1)}, f32[16,384]{1,0:T(8,128)S(1)}) all-reduce(f32[16,384]{1,0:T(8,128)S(1)} %fusion.8, f32[16,384]{1,0:T(8,128)S(1)} %fusion.11), channel_id=1, replica_groups=mesh['groups'=2,'dp'=2,'tensor'=8] {'tensor'}, use_global_device_ids=true, to_apply=%region_3.4 | all-reduce | flops 12288 | bytes 98304 | tf_op jit(solution)/shard_map/psum | solution.py:45
  48.5 4.0 %convolution_convert_fusion.1 = bf16[32,16,2048]{2,1,0:T(8,128)(2,1)} fusion(bf16[384,2048]{1,0:T(8,128)(2,1)} %param.6, f32[16,384]{1,0:T(8,128)S(1)} %fusion.23, f32[32,384]{1,0:T(8,128)S(1)} %and_convert_fusion), kind=kOutput, calls=%fused_computation.3 | convolution fusion | flops 806748160 | bytes 3743744 | tf_op jit(solution)/shard_map/dot_general | solution.py:70
  52.5 1.7 convolution_convert_fusion.2
  54.2 0.0 all-gather.2.cloned.1.call-start
  54.3 0.5 all-gather.2.cloned.1.call-update
  54.8 0.2 reduce-scatter.2.cloned.1.call-start
  55.0 26.5 %convolution_convert_fusion = bf16[8192,384]{1,0:T(8,128)(2,1)} fusion(bf16[2048,8192]{1,0:T(8,128)(2,1)} %param.7, bf16[384,2048]{1,0:T(8,128)(2,1)} %param.6), kind=kOutput, calls=%fused_computation | convolution fusion | flops 12888047616 | bytes 41418752 | tf_op jit(solution)/shard_map/dot_general | solution.py:53
  81.5 0.0 all-reduce.4.cloned.1.call-done
  81.6 2.1 dynamic-slice_convert_fusion.1
  83.7 2.8 dynamic-slice_convert_fusion
  86.5 67.8 %all-gather.2.cloned.1.call-done = bf16[384,8192]{1,0:T(8,128)(2,1)} async-done(((bf16[384,1024]{1,0:T(8,128)(2,1)}), bf16[384,8192]{1,0:T(8,128)(2,1)}) %all-gather.2.cloned.1.call-update) | async-done | bytes 6291472 | tf_op jit(solution)/shard_map/all_gather | solution.py:83
  154.4 21.0 %fusion.24 = f32[384,2048]{1,0:T(8,128)} fusion(bf16[384,8192]{1,0:T(8,128)(2,1)} %all-gather.2.cloned.1.call-done, bf16[2048,8192]{1,0:T(8,128)(2,1)} %param.7), kind=kOutput, calls=%fused_computation.34 | convolution fusion | flops 12884901888 | bytes 42991616 | tf_op jit(solution)/shard_map/dot_general | solution.py:82
  175.4 4.1 %fusion = bf16[384,2048]{1,0:T(8,128)(2,1)} fusion(f32[384,2048]{1,0:T(8,128)} %fusion.24, bf16[32,16,2048]{2,1,0:T(8,128)(2,1)S(1)} %copy-done, f32[16,384]{1,0:T(8,128)S(1)} %fusion.23, f32[32,384]{1,0:T(8,128)S(1)} %and_convert_fusion), kind=kOutput, calls=%fused_computation.2 | convolution fusion | flops 807272448 | bytes 6889472 | tf_op jit(solution)/shard_map/dot_general | solution.py:88
  179.4 94.9 %reduce-scatter.2.cloned.1.call-done = bf16[1024,384]{1,0:T(8,128)(2,1)} async-done(((bf16[8192,384]{1,0:T(8,128)(2,1)}), bf16[1024,384]{1,0:T(8,128)(2,1)}) %reduce-scatter.2.cloned.1.call-update) | async-done | bytes 786448 | tf_op jit(solution)/shard_map/reduce_scatter | solution.py:52
  274.3 2.2 fusion.1
  276.5 1.2 copy.23
  (11 shorter events, 0.1 us)
Async XLA Ops:
  8.0 1.9 copy-start
  8.0 73.5 %all-reduce.4.cloned.1.call-start = ((), (), s32[]{:S(2)}) async-start(), calls=%async_computation.3 | async-start | bytes 6291456 | tf_op jit(solution)/shard_map/psum | solution.py:74
  9.9 2.8 copy-start.1
  9.9 2.8 copy-start.2
  54.2 100.1 %all-gather.2.cloned.1.call-start = ((), (), s32[]{:S(2)}) async-start(), calls=%async_computation.2 | async-start | bytes 7077888 | tf_op jit(solution)/shard_map/all_gather | solution.py:83
  54.8 219.5 %reduce-scatter.2.cloned.1.call-start = ((), (), s32[]{:S(2)}) async-start(), calls=%async_computation.1 | async-start | bytes 7077888 | tf_op jit(solution)/shard_map/reduce_scatter | solution.py:52
Sparse Core Ops, SparseCore 0:
  54.3 23.5 all-reduce.3
Sparse Core Ops, SparseCore 1:
  56.9 97.4 all-gather.1
  157.8 116.5 reduce-scatter.1
where the time goes:
time: 288 us; the launch traced here: 285 us
  waiting for transfers between devices  163 us (57%)
  matrix products  63 us (22%)
  blocking collectives  35.1 us (12%)
  between operations  15.6 us (5%)
  other arithmetic  5.88 us (2%)
    reduce_scatter x1, waiting for transfers between devices, body(): lax.psum_scatter(lax.dot_general(weight_cols, hidden, cross, preferred_el...  94.9 us
    all_gather x1, waiting for transfers between devices, body(): lax.all_gather(output_gradient, 'tensor', axis=1, tiled=True)  67.8 us
    psum x1, blocking collectives, body(): low = lax.psum(low_part, 'tensor')  35.1 us
    dot_general x1, matrix products, body(): lax.dot_general(weight_cols, hidden, cross, preferred_element_type=jnp.fl...  26.5 us
    dot_general x1, matrix products, body(): lax.dot_general(lax.all_gather(output_gradient, 'tensor', axis=1, tiled=T...  21 us
  transfers between devices with their start and end apart: 3, of which 2 were waited for; matrix products, arithmetic and copies ran while one was open for 20% of the time, Pallas kernels for 0%

commit v1 on v0

--- a/solution.py
+++ b/solution.py
@@ -1,6 +1,8 @@
 import jax
 import jax.numpy as jnp
 from jax import lax
+from jax.experimental import pallas as pl
+from jax.experimental.pallas import tpu as pltpu
 from jax.sharding import PartitionSpec as P
 
 SCALE = 2.0
@@ -92,6 +94,466 @@
     return (mixed, grad_hidden, grad_a, grad_b)
 
 
+Z, Y = 4, 2
+MESH = pl.DeviceIdType.MESH
+F32, BF16 = jnp.float32, jnp.bfloat16
+
+
+def fused_kernel(
+    job_ref, hidden_ref, in_ref, out_ref, og_ref, w_ref,
+    mixed_ref, gh_ref, ga_ref, gb_ref,
+    gat, part, wbuf, acc, adp, ray, raz, rbz, rby, xs, xr, lw, bw, gsend_a, gsend_b, grecv_a, grecv_b,
+    wsem, azs, azr, ays, ayr, bys, byr, bzs, bzr,
+    rays, rayr, razs, razr, rbzs, rbzr, rbys, rbyr, xss, xrs, gss, grs,
+):
+    rows, lh = hidden_ref.shape
+    lwid = og_ref.shape[1]
+    wide = in_ref.shape[0]
+    ra, rb = ray.shape[1], rby.shape[0]
+    sa, sb = pl.ds(0, ra), pl.ds(ra, rb)
+    half = ga_ref.shape[0]
+    dp = lax.axis_index("dp")
+    t = lax.axis_index("tensor")
+    z, y = t // Y, t % Y
+    oy = 1 - y
+    tl, tr, ty = jnp.maximum(t - Y, 0), jnp.minimum(t + Y, Z * Y - 1), z * Y + oy
+    t1, t2 = (z + 1 - 2 * (z % 2)) * Y + y, ((z + 2) % Z) * Y + y
+    hop = (tr, tl)
+
+    def cp(a, b, ss, rs, dst):
+        return pltpu.make_async_remote_copy(
+            src_ref=a, dst_ref=b, send_sem=ss, recv_sem=rs,
+            device_id={"tensor": dst}, device_id_type=MESH)
+
+    def cpd(a, b, ss, rs):
+        return pltpu.make_async_remote_copy(
+            src_ref=a, dst_ref=b, send_sem=ss, recv_sem=rs,
+            device_id={"dp": 1 - dp}, device_id_type=MESH)
+
+    col = (y, oy)
+
+    def ag_az(d, zs, own=False):
+        s = zs * Y + y
+        a = og_ref.at[sa] if own else gat.at[s, sa]
+        return cp(a, gat.at[s, sa], azs.at[d, zs], azr.at[zs], hop[d])
+
+    def ag_ay(zs, own=False):
+        s = zs * Y + y
+        a = og_ref.at[sa] if own else gat.at[s, sa]
+        return cp(a, gat.at[s, sa], ays.at[zs], ayr.at[zs], ty)
+
+    def ag_by():
+        return cp(og_ref.at[sb], gat.at[t, sb], bys, byr, ty)
+
+    def ag_bz(d, zs, rel, own=False):
+        s = zs * Y + col[rel]
+        a = og_ref.at[sb] if own else gat.at[s, sb]
+        return cp(a, gat.at[s, sb], bzs.at[d, zs, rel], bzr.at[zs, rel], hop[d])
+
+    def rs_ay(d):
+        return cp(part.at[d * Y + oy, sa], ray.at[d], rays.at[d], rayr.at[d], ty)
+
+    def rs_az(k, d):
+        return cp(part.at[d * Y + y, sa], raz.at[k, d], razs.at[k, d], razr.at[k, d], hop[k])
+
+    def rs_bz(k, d, rel):
+        return cp(part.at[d * Y + col[rel], sb], rbz.at[k, d, rel], rbzs.at[k, d, rel],
+                  rbzr.at[k, d, rel], hop[k])
+
+    def rs_by():
+        return cp(part.at[z * Y + oy, sb], rby, rbys, rbyr, ty)
+
+    def exch(i):
+        return cp(xs.at[i], xr.at[i], xss.at[i], xrs.at[i], (ty, t1, t2)[i])
+
+    def block_of(s):
+        q = (s % (Z * Y)) // Y
+        r = s % Y
+        low_z = z < Z // 2
+        far = jnp.where(low_z, Z - 1 - q, q)
+        zm = jnp.where(low_z, z, Z - 1 - z)
+        near = jnp.where((zm == 1) & (q < 2), 1 - q, q)
+        near = jnp.where(low_z, near, Z - 1 - near)
+        first = s < Z * Y
+        zz = jnp.where(first, far, near)
+        return zz, jnp.where(first, jnp.where(r == 0, oy, y), jnp.where(r == 0, y, oy))
+
+    slots = wbuf.shape[0]
+
+    def wcopy(s):
+        zz, yy = block_of(s)
+        c = pl.multiple_of((zz * Y + yy) * lwid, lwid)
+        return pltpu.make_async_copy(
+            w_ref.at[:, pl.ds(c, lwid)], wbuf.at[s % slots], wsem.at[s % slots])
+
+    steps = 2 * Z * Y
+
+    barrier = pltpu.get_barrier_semaphore()
+
+    def greet(**dev):
+        pl.semaphore_signal(barrier, inc=1, device_id=dev, device_id_type=MESH)
+
+    greet(tensor=ty)
+    greet(tensor=t2)
+    greet(dp=1 - dp)
+
+    @pl.when(z > 0)
+    def _():
+        greet(tensor=tl)
+
+    @pl.when(z < Z - 1)
+    def _():
+        greet(tensor=tr)
+
+    wcopy(0).start()
+    wcopy(1).start()
+    inner = (z > 0) & (z < Z - 1)
+
+    @pl.when(inner)
+    def _():
+        pl.semaphore_wait(barrier, 5)
+
+    @pl.when(jnp.logical_not(inner))
+    def _():
+        pl.semaphore_wait(barrier, 4)
+
+    has = (z < Z - 1, z > 0)
+    from_side = (z > 0, z < Z - 1)
+    ag_by().start()
+    for k in range(2):
+        @pl.when(has[k])
+        def _(k=k):
+            ag_az(k, z, True).start()
+            ag_bz(k, z, 0, True).start()
+    ag_ay(z, True).start()
+
+    gat[t] = og_ref[...]
+
+    tile = 128
+    jobs = tile // 16
+    job = job_ref[...]
+
+    def mask_of(n):
+        r = lax.broadcasted_iota(jnp.int32, (tile, rows), 0) + n * tile
+        return (r // 16) == job
+
+    nt = (((1,), (1,)), ((), ()))
+    tn = (((0,), (0,)), ((), ()))
+
+    def low_tile(a_ref, b_ref, n):
+        v = lax.dot_general(a_ref[pl.ds(pl.multiple_of(n * tile, tile), tile), :], b_ref[...], nt,
+                            preferred_element_type=F32)
+        v = jnp.where(mask_of(n), v, 0.0)
+        return jnp.sum(v.reshape(jobs, 16, rows), axis=0)
+
+    zero = jnp.zeros((16, rows), F32)
+
+    xs[0, pl.ds(0, 16)] = lax.fori_loop(
+        0, wide // tile, lambda n, c: c + low_tile(in_ref, hidden_ref, n), zero)
+    xs[0, pl.ds(16, 16)] = lax.fori_loop(
+        0, wide // tile, lambda n, c: c + low_tile(out_ref, og_ref, n), zero)
+    exch(0).start()
+
+    nw = 256
+
+    def next_w(s):
+        wcopy(s).wait()
+
+        @pl.when(s + 2 < steps)
+        def _():
+            wcopy(s + 2).start()
+
+    def forward_step(s, c):
+        next_w(s)
+        zz, yy = block_of(s)
+        slot = s % slots
+        b = zz * Y + yy
+
+        def inner_tile(n, c):
+            cs = pl.ds(pl.multiple_of(n * nw, nw), nw)
+            part[b, :, cs] = jnp.dot(
+                hidden_ref[...], wbuf[slot, :, cs], preferred_element_type=F32).astype(BF16)
+            return c
+
+        lax.fori_loop(0, lwid // nw, inner_tile, 0)
+
+        @pl.when(s % Y == 0)
+        def _():
+            rs_ay(zz).start()
+        return c
+
+    def back_step(s):
+        next_w(s)
+        zz, yy = block_of(s)
+        slot = s % slots
+        b = zz * Y + yy
+
+        def inner_tile(n, c):
+            cs = pl.ds(pl.multiple_of(n * nw, nw), nw)
+            acc[:, cs] += lax.dot_general(
+                gat[b], wbuf[slot, cs, :], nt, preferred_element_type=F32)
+            return c
+
+        lax.fori_loop(0, lh // nw, inner_tile, 0)
+
+    step_rows = 48
+
+    def add_into(dst, srcs, n):
+        def go(i, c):
+            rs = pl.ds(pl.multiple_of(i * step_rows, step_rows), step_rows)
+            v = dst[rs, :].astype(F32)
+            for x in srcs:
+                v = v + x[rs, :].astype(F32)
+            dst[rs, :] = v.astype(dst.dtype)
+            return c
+        lax.fori_loop(0, n // step_rows, go, 0)
+
+    def ag_round(k):
+        for d in range(2):
+            zs = z - k if d == 0 else z + k
+            ok = zs >= 0 if d == 0 else zs < Z
+            zc = jnp.clip(zs, 0, Z - 1)
+
+            @pl.when(ok)
+            def _(d=d, zc=zc):
+                ag_az(d, zc).wait_recv()
+
+                @pl.when(has[d])
+                def _():
+                    ag_az(d, zc).start()
+                ag_ay(zc).start()
+        for rel in range(2):
+            for d in range(2):
+                zs = z - k if d == 0 else z + k
+                ok = zs >= 0 if d == 0 else zs < Z
+                zc = jnp.clip(zs, 0, Z - 1)
+
+                @pl.when(ok)
+                def _(d=d, zc=zc, rel=rel):
+                    ag_bz(d, zc, rel).wait_recv()
+
+                    @pl.when(has[d])
+                    def _():
+                        ag_bz(d, zc, rel).start()
+
+    def rs_round(r):
+        for k in range(2):
+            pos = z if k == 0 else Z - 1 - z
+            dd = Z - 1 - r + pos if k == 0 else r - pos
+            d = jnp.clip(dd, 0, Z - 1)
+
+            @pl.when(r >= pos)
+            def _(k=k, d=d):
+                for rel in (1, 0):
+                    @pl.when(from_side[k])
+                    def _(rel=rel):
+                        rs_bz(k, d, rel).wait_recv()
+                        add_into(part.at[d * Y + col[rel], sb], [rbz.at[k, d, rel]], rb)
+                    rs_bz(k, d, rel).start()
+                rs_ay(d).wait_recv()
+
+                @pl.when(from_side[k])
+                def _():
+                    rs_az(k, d).wait_recv()
+                    add_into(part.at[d * Y + y, sa], [ray.at[d], raz.at[k, d]], ra)
+
+                @pl.when(jnp.logical_not(from_side[k]))
+                def _():
+                    add_into(part.at[d * Y + y, sa], [ray.at[d]], ra)
+                rs_az(k, d).start()
+
+    lax.fori_loop(0, Z, forward_step, 0)
+    ag_by().wait_recv()
+    for k in range(2):
+        @pl.when(has[k])
+        def _(k=k):
+            ag_bz(k, z, 1).start()
+    exch(0).wait_recv()
+    xs[1] = xs[0] + xr[0]
+    exch(1).start()
+    lax.fori_loop(Z, 2 * Z, forward_step, 0)
+    exch(1).wait_recv()
+    xs[2] = xs[1] + xr[1]
+    exch(2).start()
+    rs_round(0)
+    ag_round(1)
+    exch(2).wait_recv()
+    low = SCALE * (xs[2, pl.ds(0, 16)] + xr[2, pl.ds(0, 16)])
+    back = SCALE * (xs[2, pl.ds(16, 16)] + xr[2, pl.ds(16, 16)])
+    low8 = jnp.concatenate([low] * jobs, axis=0)
+    back8 = jnp.concatenate([back] * jobs, axis=0)
+    for n in range(wide // tile):
+        m = mask_of(n)
+        lw[pl.ds(n * tile, tile), :] = jnp.where(m, low8, 0.0).astype(BF16)
+        bw[pl.ds(n * tile, tile), :] = jnp.where(m, back8, 0.0).astype(BF16)
+
+    theirs = pl.ds(pl.multiple_of((1 - dp) * half, half), half)
+    mine = pl.ds(pl.multiple_of(dp * half, half), half)
+    gtile = 256
+
+    def cols_loop(n, f):
+        def go(i, c):
+            f(pl.ds(pl.multiple_of(i * gtile, gtile), gtile))
+            return c
+        lax.fori_loop(0, n // gtile, go, 0)
+
+    def send_a(cs):
+        gsend_a[:, cs] = jnp.dot(bw[theirs, :], hidden_ref[:, cs], preferred_element_type=F32).astype(BF16)
+
+    def send_b(cs):
+        gsend_b[:, cs] = jnp.dot(lw[theirs, :], og_ref[:, cs], preferred_element_type=F32).astype(BF16)
+
+    def init_acc(cs):
+        acc[:, cs] = lax.dot_general(bw[...], in_ref[:, cs], tn, preferred_element_type=F32)
+
+    def init_adp(cs):
+        adp[:, cs] = lax.dot_general(lw[...], out_ref[:, cs], tn, preferred_element_type=F32)
+
+    g_a = cpd(gsend_a, grecv_a, gss.at[0], grs.at[0])
+    g_b = cpd(gsend_b, grecv_b, gss.at[1], grs.at[1])
+    cols_loop(lh, send_a)
+    g_a.start()
+    cols_loop(lwid, send_b)
+    g_b.start()
+    cols_loop(lh, init_acc)
+
+    def back_pair(q):
+        s = Z * Y + q * Y
+        back_step(s)
+        zz, _ = block_of(s)
+        ag_ay(zz).wait_recv()
+        back_step(s + 1)
+
+    back_pair(0)
+    rs_round(1)
+    ag_round(2)
+    cols_loop(lwid, init_adp)
+
+    g_a.wait_recv()
+    g_b.wait_recv()
+
+    def own_a(cs):
+        ga_ref[:, cs] = jnp.dot(bw[mine, :], hidden_ref[:, cs], preferred_element_type=F32) + grecv_a[:, cs].astype(F32)
+
+    def own_b(cs):
+        gb_ref[:, cs] = jnp.dot(lw[mine, :], og_ref[:, cs], preferred_element_type=F32) + grecv_b[:, cs].astype(F32)
+
+    cols_loop(lh, own_a)
+    cols_loop(lwid, own_b)
+    back_pair(1)
+    rs_round(2)
+    ag_round(3)
+    back_pair(2)
+
+    for k in range(2):
+        @pl.when(from_side[k])
+        def _(k=k):
+            rs_bz(k, z, 1).wait_recv()
+            add_into(part.at[z * Y + oy, sb], [rbz.at[k, z, 1]], rb)
+    rs_by().start()
+    rs_ay(z).wait_recv()
+    add_into(adp.at[sa], [part.at[t, sa], ray.at[z]], ra)
+    add_into(adp.at[sb], [part.at[t, sb]], rb)
+    for k in range(2):
+        @pl.when(from_side[k])
+        def _(k=k):
+            rs_bz(k, z, 0).wait_recv()
+            add_into(adp.at[sb], [rbz.at[k, z, 0]], rb)
+            rs_az(k, z).wait_recv()
+            add_into(adp.at[sa], [raz.at[k, z]], ra)
+    back_pair(3)
+
+    def end_gh(cs):
+        gh_ref[:, cs] = acc[:, cs].astype(BF16)
+
+    cols_loop(lh, end_gh)
+    rs_by().wait_recv()
+    add_into(adp.at[sb], [rby], rb)
+
+    def end_mixed(cs):
+        mixed_ref[:, cs] = adp[:, cs].astype(BF16)
+
+    cols_loop(lwid, end_mixed)
+
+    g_a.wait_send()
+    g_b.wait_send()
+    ag_by().wait_send()
+    rs_by().wait_send()
+    for i in range(3):
+        exch(i).wait_send()
+    for d in range(Z):
+        ag_ay(d).wait_send()
+        rs_ay(d).wait_send()
+        for k in range(2):
+            @pl.when((d <= z if k == 0 else d >= z) & has[k])
+            def _(k=k, d=d):
+                ag_az(k, d).wait_send()
+                ag_bz(k, d, 0).wait_send()
+                ag_bz(k, d, 1).wait_send()
+
+            @pl.when(d > z if k == 0 else d < z)
+            def _(k=k, d=d):
+                rs_az(k, d).wait_send()
+                rs_bz(k, d, 0).wait_send()
+                rs_bz(k, d, 1).wait_send()
+
+
+def fused_body(hidden, down_matrix, rank_input_map, rank_output_map, job_row_counts, output_gradient):
+    rows, lh = hidden.shape
+    job_count, rank_count, lwid = rank_output_map.shape
+    wide = job_count * rank_count
+    positions = lax.axis_index("dp") * rows + lax.iota(jnp.int32, rows)
+    ends = jnp.cumsum(job_row_counts)
+    job = jnp.sum((ends[:, None] <= positions[None, :]).astype(jnp.int32), axis=0)[None, :]
+    rb = (rows * 3 // 8) // 48 * 48
+    ra = rows - rb
+    n = Z * Y
+    half = wide // 2
+    dma = pltpu.SemaphoreType.DMA
+    vm = pl.BlockSpec(memory_space=pltpu.VMEM)
+    mixed, gh, ga, gb = pl.pallas_call(
+        fused_kernel,
+        out_shape=(
+            jax.ShapeDtypeStruct((rows, lwid), BF16),
+            jax.ShapeDtypeStruct((rows, lh), BF16),
+            jax.ShapeDtypeStruct((half, lh), F32),
+            jax.ShapeDtypeStruct((half, lwid), F32),
+        ),
+        in_specs=[vm, vm, vm, vm, vm, pl.BlockSpec(memory_space=pl.ANY)],
+        out_specs=(vm, vm, vm, vm),
+        scratch_shapes=[
+            pltpu.VMEM((n, rows, lwid), BF16),
+            pltpu.VMEM((n, rows, lwid), BF16),
+            pltpu.VMEM((3, lh, lwid), BF16),
+            pltpu.VMEM((rows, lh), F32),
+            pltpu.VMEM((rows, lwid), F32),
+            pltpu.VMEM((Z, ra, lwid), BF16),
+            pltpu.VMEM((2, Z, ra, lwid), BF16),
+            pltpu.VMEM((2, Z, 2, rb, lwid), BF16),
+            pltpu.VMEM((rb, lwid), BF16),
+            pltpu.VMEM((3, 2 * rank_count, rows), F32),
+            pltpu.VMEM((3, 2 * rank_count, rows), F32),
+            pltpu.VMEM((wide, rows), BF16),
+            pltpu.VMEM((wide, rows), BF16),
+            pltpu.VMEM((half, lh), BF16),
+            pltpu.VMEM((half, lwid), BF16),
+            pltpu.VMEM((half, lh), BF16),
+            pltpu.VMEM((half, lwid), BF16),
+            dma((3,)),
+            dma((2, Z)), dma((Z,)), dma((Z,)), dma((Z,)), dma, dma, dma((2, Z, 2)), dma((Z, 2)),
+            dma((Z,)), dma((Z,)), dma((2, Z)), dma((2, Z)), dma((2, Z, 2)), dma((2, Z, 2)), dma, dma,
+            dma((3,)), dma((3,)), dma((2,)), dma((2,)),
+        ],
+        compiler_params=pltpu.CompilerParams(
+            collective_id=0, has_side_effects=True, vmem_limit_bytes=62 * 1024 * 1024),
+    )(
+        job, hidden, rank_input_map.reshape(wide, lh), rank_output_map.reshape(wide, lwid),
+        output_gradient, down_matrix,
+    )
+    share = job_count // 2
+    return mixed, gh, ga.reshape(share, rank_count, lh), gb.reshape(share, rank_count, lwid)
+
+
 def solution(mesh):
     placed = (
         P(("groups", "dp"), "tensor"),
@@ -102,7 +564,7 @@
         P(("groups", "dp"), "tensor"),
     )
     return jax.shard_map(
-        body,
+        fused_body if mesh.shape["tensor"] == Z * Y else body,
         mesh=mesh,
         in_specs=placed,
         out_specs=(

time: 288 us -> 135 us (0.47)
  waiting for transfers between devices: 163 us -> 0 us
  Pallas kernels: 0 us -> 126 us
  matrix products: 63 us -> 0 us
  blocking collectives: 35.1 us -> 0 us
  between operations: 15.6 us -> 0.67 us
  other arithmetic: 5.88 us -> 0.27 us
  local copies, waits for them, and re-layouts: 2.07 us -> 7.6 us
    pallas_call x0 -> x1, Pallas kernels: none -> 126 us  [fused_body(): pl.pallas_call(fused_kernel, out_shape=(jax.ShapeDtypeStruct((rows, lwid)...]
    reduce_scatter x1 -> x0, waiting for transfers between devices: 94.9 us -> none  [body(): lax.psum_scatter(lax.dot_general(weight_cols, hidden, cross, preferred_el...]
    all_gather x1 -> x0, waiting for transfers between devices: 67.8 us -> none  [body(): lax.all_gather(output_gradient, 'tensor', axis=1, tiled=True)]
    dot_general x8 -> x0, matrix products: 63 us -> none  [the longest x1 26.5 us: body(): lax.dot_general(weight_cols, hidden, cross, preferred_element_type=jnp.fl...]
    psum x1 -> x0, blocking collectives: 35.1 us -> none  [body(): low = lax.psum(low_part, 'tensor')]
    unnamed x7 -> x10, local copies, waits for them, and re-layouts: 1.19 us -> 6.29 us
    convert_element_type x5 -> x0, other arithmetic: 5.04 us -> none  [the longest x1 2.81 us: body(): lax.psum(grad_a_local.astype(jnp.bfloat16), 'dp').astype(jnp.float32)]
  transfers between devices with their start and end apart: 3 -> 0, of which waited for: 2 -> 0; matrix products, arithmetic and copies ran while one was open for 20% -> 0% of each run, Pallas kernels for 0% -> 0%
where the time goes in v1:
time: 135 us
  Pallas kernels  126 us (93%)
  local copies, waits for them, and re-layouts  7.6 us (6%)
    pallas_call x1, Pallas kernels, fused_body(): pl.pallas_call(fused_kernel, out_shape=(jax.ShapeDtypeStruct((rows, lwid)...  126 us
    unnamed x10, local copies, waits for them, and re-layouts  6.29 us

profile of v1, /device:TPU:10, one launch (start us, length us, event | category | flops | bytes accessed | tf_op | source)
XLA Modules:
  0.0 134.6 jit_solution(13741272837527997989)
XLA Ops:
  0.6 0.7 copy.12
  1.4 0.1 reduce-window.8
  1.4 0.1 reduce
  1.6 0.1 convert_reduce_fusion
  1.6 0.6 broadcast_in_dim.2.job_ref
  2.2 126.1 %shard_map.93 = (bf16[384,1024]{1,0:T(8,128)(2,1)}, bf16[384,2048]{1,0:T(8,128)(2,1)}, f32[256,2048]{1,0:T(8,128)}, f32[256,1024]{1,0:T(8,128)}) custom-call(s32[1,384]{1,0:T(1,128)} %broadcast_in_dim.2.job_ref, bf16[384,2048]{1,0:T(8,128)(2,1)} %hidden_ref.1, bf16[512,2048]{1,0:T(8,128)(2,1)} %bitcast.5, bf16[512,1024]{1,0:T(8,128)(2,1)} %bitcast.7, ...), custom_call_target="tpu_custom_call" | custom-call | tf_op jit(solution)/shard_map/pallas_call | solution.py:514
  128.3 0.0 copy-start.1
  128.3 0.0 copy-start
  128.3 2.2 %copy.17 = bf16[384,1024]{1,0:T(8,128)(2,1)} copy(bf16[384,1024]{1,0:T(8,128)(2,1)} %get-tuple-element.16) | data formatting | bytes 1572864
  130.6 0.0 copy-done.1
  130.6 1.1 copy.18
  131.7 0.0 copy-done
  131.7 0.0 copy-start.2
  131.7 1.3 copy.19
  133.0 0.6 copy-done.2
  133.7 1.0 copy.20
  (1 shorter events, 0.0 us)
Async XLA Ops:
  128.3 2.2 %copy-start.1 = (bf16[384,2048]{1,0:T(8,128)(2,1)S(1)}, bf16[384,2048]{1,0:T(8,128)(2,1)}, u32[]{:S(2)}) copy-start(bf16[384,2048]{1,0:T(8,128)(2,1)} %get-tuple-element.17) | copy-start | bytes 4718596
  128.3 3.4 %copy-start = (f32[256,2048]{1,0:T(8,128)S(1)}, f32[256,2048]{1,0:T(8,128)}, u32[]{:S(2)}) copy-start(f32[256,2048]{1,0:T(8,128)} %get-tuple-element.10) | copy-start | bytes 6291460
  131.7 2.0 %copy-start.2 = (f32[256,1024]{1,0:T(8,128)S(1)}, f32[256,1024]{1,0:T(8,128)}, u32[]{:S(2)}) copy-start(f32[256,1024]{1,0:T(8,128)} %get-tuple-element.11) | copy-start | bytes 3145732

commit v2 on v1

--- a/solution.py
+++ b/solution.py
@@ -95,6 +95,7 @@
 
 
 Z, Y = 4, 2
+CHUNKS = 2
 MESH = pl.DeviceIdType.MESH
 F32, BF16 = jnp.float32, jnp.bfloat16
 
@@ -110,7 +111,10 @@
     lwid = og_ref.shape[1]
     wide = in_ref.shape[0]
     ra, rb = ray.shape[1], rby.shape[0]
-    sa, sb = pl.ds(0, ra), pl.ds(ra, rb)
+    rac, rbc = ra // CHUNKS, rb // CHUNKS
+    sa = [pl.ds(c * rac, rac) for c in range(CHUNKS)]
+    sb = [pl.ds(ra + c * rbc, rbc) for c in range(CHUNKS)]
+    sb0 = [pl.ds(c * rbc, rbc) for c in range(CHUNKS)]
     half = ga_ref.shape[0]
     dp = lax.axis_index("dp")
     t = lax.axis_index("tensor")
@@ -132,36 +136,37 @@
 
     col = (y, oy)
 
-    def ag_az(d, zs, own=False):
+    def ag_az(c, d, zs, own=False):
         s = zs * Y + y
-        a = og_ref.at[sa] if own else gat.at[s, sa]
-        return cp(a, gat.at[s, sa], azs.at[d, zs], azr.at[zs], hop[d])
-
-    def ag_ay(zs, own=False):
+        a = og_ref.at[sa[c]] if own else gat.at[s, sa[c]]
+        return cp(a, gat.at[s, sa[c]], azs.at[d, zs, c], azr.at[zs, c], hop[d])
+
+    def ag_ay(c, zs, own=False):
         s = zs * Y + y
-        a = og_ref.at[sa] if own else gat.at[s, sa]
-        return cp(a, gat.at[s, sa], ays.at[zs], ayr.at[zs], ty)
-
-    def ag_by():
-        return cp(og_ref.at[sb], gat.at[t, sb], bys, byr, ty)
-
-    def ag_bz(d, zs, rel, own=False):
+        a = og_ref.at[sa[c]] if own else gat.at[s, sa[c]]
+        return cp(a, gat.at[s, sa[c]], ays.at[zs, c], ayr.at[zs, c], ty)
+
+    def ag_by(c):
+        return cp(og_ref.at[sb[c]], gat.at[t, sb[c]], bys.at[c], byr.at[c], ty)
+
+    def ag_bz(c, d, zs, rel, own=False):
         s = zs * Y + col[rel]
-        a = og_ref.at[sb] if own else gat.at[s, sb]
-        return cp(a, gat.at[s, sb], bzs.at[d, zs, rel], bzr.at[zs, rel], hop[d])
-
-    def rs_ay(d):
-        return cp(part.at[d * Y + oy, sa], ray.at[d], rays.at[d], rayr.at[d], ty)
-
-    def rs_az(k, d):
-        return cp(part.at[d * Y + y, sa], raz.at[k, d], razs.at[k, d], razr.at[k, d], hop[k])
-
-    def rs_bz(k, d, rel):
-        return cp(part.at[d * Y + col[rel], sb], rbz.at[k, d, rel], rbzs.at[k, d, rel],
-                  rbzr.at[k, d, rel], hop[k])
-
-    def rs_by():
-        return cp(part.at[z * Y + oy, sb], rby, rbys, rbyr, ty)
+        a = og_ref.at[sb[c]] if own else gat.at[s, sb[c]]
+        return cp(a, gat.at[s, sb[c]], bzs.at[d, zs, rel, c], bzr.at[zs, rel, c], hop[d])
+
+    def rs_ay(c, d):
+        return cp(part.at[d * Y + oy, sa[c]], ray.at[d, sa[c]], rays.at[d, c], rayr.at[d, c], ty)
+
+    def rs_az(c, k, d):
+        return cp(part.at[d * Y + y, sa[c]], raz.at[k, d, sa[c]], razs.at[k, d, c],
+                  razr.at[k, d, c], hop[k])
+
+    def rs_bz(c, k, d, rel):
+        return cp(part.at[d * Y + col[rel], sb[c]], rbz.at[k, d, rel, sb0[c]], rbzs.at[k, d, rel, c],
+                  rbzr.at[k, d, rel, c], hop[k])
+
+    def rs_by(c):
+        return cp(part.at[z * Y + oy, sb[c]], rby.at[sb0[c]], rbys.at[c], rbyr.at[c], ty)
 
     def exch(i):
         return cp(xs.at[i], xr.at[i], xss.at[i], xrs.at[i], (ty, t1, t2)[i])
@@ -219,13 +224,15 @@
 
     has = (z < Z - 1, z > 0)
     from_side = (z > 0, z < Z - 1)
-    ag_by().start()
-    for k in range(2):
-        @pl.when(has[k])
-        def _(k=k):
-            ag_az(k, z, True).start()
-            ag_bz(k, z, 0, True).start()
-    ag_ay(z, True).start()
+    for c in range(CHUNKS):
+        ag_by(c).start()
+    for c in range(CHUNKS):
+        for k in range(2):
+            @pl.when(has[k])
+            def _(k=k, c=c):
+                ag_az(c, k, z, True).start()
+                ag_bz(c, k, z, 0, True).start()
+        ag_ay(c, z, True).start()
 
     gat[t] = og_ref[...]
 
@@ -279,10 +286,11 @@
 
         @pl.when(s % Y == 0)
         def _():
-            rs_ay(zz).start()
+            for p in range(CHUNKS):
+                rs_ay(p, zz).start()
         return c
 
-    def back_step(s):
+    def back_step(s, last=False):
         next_w(s)
         zz, yy = block_of(s)
         slot = s % slots
@@ -290,13 +298,17 @@
 
         def inner_tile(n, c):
             cs = pl.ds(pl.multiple_of(n * nw, nw), nw)
-            acc[:, cs] += lax.dot_general(
+            v = acc[:, cs] + lax.dot_general(
                 gat[b], wbuf[slot, cs, :], nt, preferred_element_type=F32)
+            if last:
+                gh_ref[:, cs] = v.astype(BF16)
+            else:
+                acc[:, cs] = v
             return c
 
         lax.fori_loop(0, lh // nw, inner_tile, 0)
 
-    step_rows = 48
+    step_rows = 16
 
     def add_into(dst, srcs, n):
         def go(i, c):
@@ -309,65 +321,68 @@
         lax.fori_loop(0, n // step_rows, go, 0)
 
     def ag_round(k):
-        for d in range(2):
-            zs = z - k if d == 0 else z + k
-            ok = zs >= 0 if d == 0 else zs < Z
-            zc = jnp.clip(zs, 0, Z - 1)
-
-            @pl.when(ok)
-            def _(d=d, zc=zc):
-                ag_az(d, zc).wait_recv()
-
-                @pl.when(has[d])
-                def _():
-                    ag_az(d, zc).start()
-                ag_ay(zc).start()
-        for rel in range(2):
+        for c in range(CHUNKS):
             for d in range(2):
                 zs = z - k if d == 0 else z + k
                 ok = zs >= 0 if d == 0 else zs < Z
                 zc = jnp.clip(zs, 0, Z - 1)
 
                 @pl.when(ok)
-                def _(d=d, zc=zc, rel=rel):
-                    ag_bz(d, zc, rel).wait_recv()
+                def _(d=d, zc=zc, c=c):
+                    ag_az(c, d, zc).wait_recv()
 
                     @pl.when(has[d])
                     def _():
-                        ag_bz(d, zc, rel).start()
+                        ag_az(c, d, zc).start()
+                    ag_ay(c, zc).start()
+            for rel in range(2):
+                for d in range(2):
+                    zs = z - k if d == 0 else z + k
+                    ok = zs >= 0 if d == 0 else zs < Z
+                    zc = jnp.clip(zs, 0, Z - 1)
+
+                    @pl.when(ok)
+                    def _(d=d, zc=zc, rel=rel, c=c):
+                        ag_bz(c, d, zc, rel).wait_recv()
+
+                        @pl.when(has[d])
+                        def _():
+                            ag_bz(c, d, zc, rel).start()
 
     def rs_round(r):
+        for c in range(CHUNKS):
+            for k in range(2):
+                pos = z if k == 0 else Z - 1 - z
+                dd = Z - 1 - r + pos if k == 0 else r - pos
+                d = jnp.clip(dd, 0, Z - 1)
+
+                @pl.when(r >= pos)
+                def _(k=k, d=d, c=c):
+                    for rel in (1, 0):
+                        @pl.when(from_side[k])
+                        def _(rel=rel):
+                            rs_bz(c, k, d, rel).wait_recv()
+                            add_into(part.at[d * Y + col[rel], sb[c]], [rbz.at[k, d, rel, sb0[c]]], rbc)
+                        rs_bz(c, k, d, rel).start()
+                    rs_ay(c, d).wait_recv()
+
+                    @pl.when(from_side[k])
+                    def _():
+                        rs_az(c, k, d).wait_recv()
+                        add_into(part.at[d * Y + y, sa[c]], [ray.at[d, sa[c]], raz.at[k, d, sa[c]]], rac)
+
+                    @pl.when(jnp.logical_not(from_side[k]))
+                    def _():
+                        add_into(part.at[d * Y + y, sa[c]], [ray.at[d, sa[c]]], rac)
+                    rs_az(c, k, d).start()
+
+    lax.fori_loop(0, Z, forward_step, 0)
+    for c in range(CHUNKS):
+        ag_by(c).wait_recv()
         for k in range(2):
-            pos = z if k == 0 else Z - 1 - z
-            dd = Z - 1 - r + pos if k == 0 else r - pos
-            d = jnp.clip(dd, 0, Z - 1)
-
-            @pl.when(r >= pos)
-            def _(k=k, d=d):
-                for rel in (1, 0):
-                    @pl.when(from_side[k])
-                    def _(rel=rel):
-                        rs_bz(k, d, rel).wait_recv()
-                        add_into(part.at[d * Y + col[rel], sb], [rbz.at[k, d, rel]], rb)
-                    rs_bz(k, d, rel).start()
-                rs_ay(d).wait_recv()
-
-                @pl.when(from_side[k])
-                def _():
-                    rs_az(k, d).wait_recv()
-                    add_into(part.at[d * Y + y, sa], [ray.at[d], raz.at[k, d]], ra)
-
-                @pl.when(jnp.logical_not(from_side[k]))
-                def _():
-                    add_into(part.at[d * Y + y, sa], [ray.at[d]], ra)
-                rs_az(k, d).start()
-
-    lax.fori_loop(0, Z, forward_step, 0)
-    ag_by().wait_recv()
-    for k in range(2):
-        @pl.when(has[k])
-        def _(k=k):
-            ag_bz(k, z, 1).start()
+            @pl.when(has[k])
+            def _(k=k, c=c):
+                ag_bz(c, k, z, 1).start()
     exch(0).wait_recv()
     xs[1] = xs[0] + xr[0]
     exch(1).start()
@@ -421,8 +436,9 @@
         s = Z * Y + q * Y
         back_step(s)
         zz, _ = block_of(s)
-        ag_ay(zz).wait_recv()
-        back_step(s + 1)
+        for c in range(CHUNKS):
+            ag_ay(c, zz).wait_recv()
+        back_step(s + 1, q == Z - 1)
 
     back_pair(0)
     rs_round(1)
@@ -445,30 +461,28 @@
     ag_round(3)
     back_pair(2)
 
-    for k in range(2):
-        @pl.when(from_side[k])
-        def _(k=k):
-            rs_bz(k, z, 1).wait_recv()
-            add_into(part.at[z * Y + oy, sb], [rbz.at[k, z, 1]], rb)
-    rs_by().start()
-    rs_ay(z).wait_recv()
-    add_into(adp.at[sa], [part.at[t, sa], ray.at[z]], ra)
-    add_into(adp.at[sb], [part.at[t, sb]], rb)
-    for k in range(2):
-        @pl.when(from_side[k])
-        def _(k=k):
-            rs_bz(k, z, 0).wait_recv()
-            add_into(adp.at[sb], [rbz.at[k, z, 0]], rb)
-            rs_az(k, z).wait_recv()
-            add_into(adp.at[sa], [raz.at[k, z]], ra)
+    for c in range(CHUNKS):
+        for k in range(2):
+            @pl.when(from_side[k])
+            def _(k=k, c=c):
+                rs_bz(c, k, z, 1).wait_recv()
+                add_into(part.at[z * Y + oy, sb[c]], [rbz.at[k, z, 1, sb0[c]]], rbc)
+        rs_by(c).start()
+        rs_ay(c, z).wait_recv()
+        add_into(adp.at[sa[c]], [part.at[t, sa[c]], ray.at[z, sa[c]]], rac)
+        add_into(adp.at[sb[c]], [part.at[t, sb[c]]], rbc)
+        for k in range(2):
+            @pl.when(from_side[k])
+            def _(k=k, c=c):
+                rs_bz(c, k, z, 0).wait_recv()
+                add_into(adp.at[sb[c]], [rbz.at[k, z, 0, sb0[c]]], rbc)
+                rs_az(c, k, z).wait_recv()
+                add_into(adp.at[sa[c]], [raz.at[k, z, sa[c]]], rac)
     back_pair(3)
 
-    def end_gh(cs):
-        gh_ref[:, cs] = acc[:, cs].astype(BF16)
-
-    cols_loop(lh, end_gh)
-    rs_by().wait_recv()
-    add_into(adp.at[sb], [rby], rb)
+    for c in range(CHUNKS):
+        rs_by(c).wait_recv()
+        add_into(adp.at[sb[c]], [rby.at[sb0[c]]], rbc)
 
     def end_mixed(cs):
         mixed_ref[:, cs] = adp[:, cs].astype(BF16)
@@ -477,25 +491,26 @@
 
     g_a.wait_send()
     g_b.wait_send()
-    ag_by().wait_send()
-    rs_by().wait_send()
     for i in range(3):
         exch(i).wait_send()
-    for d in range(Z):
-        ag_ay(d).wait_send()
-        rs_ay(d).wait_send()
-        for k in range(2):
-            @pl.when((d <= z if k == 0 else d >= z) & has[k])
-            def _(k=k, d=d):
-                ag_az(k, d).wait_send()
-                ag_bz(k, d, 0).wait_send()
-                ag_bz(k, d, 1).wait_send()
-
-            @pl.when(d > z if k == 0 else d < z)
-            def _(k=k, d=d):
-                rs_az(k, d).wait_send()
-                rs_bz(k, d, 0).wait_send()
-                rs_bz(k, d, 1).wait_send()
+    for c in range(CHUNKS):
+        ag_by(c).wait_send()
+        rs_by(c).wait_send()
+        for d in range(Z):
+            ag_ay(c, d).wait_send()
+            rs_ay(c, d).wait_send()
+            for k in range(2):
+                @pl.when((d <= z if k == 0 else d >= z) & has[k])
+                def _(k=k, d=d, c=c):
+                    ag_az(c, k, d).wait_send()
+                    ag_bz(c, k, d, 0).wait_send()
+                    ag_bz(c, k, d, 1).wait_send()
+
+                @pl.when(d > z if k == 0 else d < z)
+                def _(k=k, d=d, c=c):
+                    rs_az(c, k, d).wait_send()
+                    rs_bz(c, k, d, 0).wait_send()
+                    rs_bz(c, k, d, 1).wait_send()
 
 
 def fused_body(hidden, down_matrix, rank_input_map, rank_output_map, job_row_counts, output_gradient):
@@ -505,11 +520,11 @@
     positions = lax.axis_index("dp") * rows + lax.iota(jnp.int32, rows)
     ends = jnp.cumsum(job_row_counts)
     job = jnp.sum((ends[:, None] <= positions[None, :]).astype(jnp.int32), axis=0)[None, :]
-    rb = (rows * 3 // 8) // 48 * 48
+    rb = (rows * 5 // 12) // (16 * CHUNKS) * (16 * CHUNKS)
     ra = rows - rb
     n = Z * Y
     half = wide // 2
-    dma = pltpu.SemaphoreType.DMA
+    dma, cs = pltpu.SemaphoreType.DMA, CHUNKS
     vm = pl.BlockSpec(memory_space=pltpu.VMEM)
     mixed, gh, ga, gb = pl.pallas_call(
         fused_kernel,
@@ -540,8 +555,10 @@
             pltpu.VMEM((half, lh), BF16),
             pltpu.VMEM((half, lwid), BF16),
             dma((3,)),
-            dma((2, Z)), dma((Z,)), dma((Z,)), dma((Z,)), dma, dma, dma((2, Z, 2)), dma((Z, 2)),
-            dma((Z,)), dma((Z,)), dma((2, Z)), dma((2, Z)), dma((2, Z, 2)), dma((2, Z, 2)), dma, dma,
+            dma((2, Z, cs)), dma((Z, cs)), dma((Z, cs)), dma((Z, cs)), dma((cs,)), dma((cs,)),
+            dma((2, Z, 2, cs)), dma((Z, 2, cs)),
+            dma((Z, cs)), dma((Z, cs)), dma((2, Z, cs)), dma((2, Z, cs)),
+            dma((2, Z, 2, cs)), dma((2, Z, 2, cs)), dma((cs,)), dma((cs,)),
             dma((3,)), dma((3,)), dma((2,)), dma((2,)),
         ],
         compiler_params=pltpu.CompilerParams(

time: 135 us -> 132 us (0.978)
  Pallas kernels: 126 us -> 123 us
    pallas_call x1, Pallas kernels: 126 us -> 123 us  [fused_body(): pl.pallas_call(fused_kernel, out_shape=(jax.ShapeDtypeStruct((rows, lwid)...]
where the time goes in v2:
time: 132 us
  Pallas kernels  123 us (93%)
  local copies, waits for them, and re-layouts  7.6 us (6%)
    pallas_call x1, Pallas kernels, fused_body(): pl.pallas_call(fused_kernel, out_shape=(jax.ShapeDtypeStruct((rows, lwid)...  123 us
    unnamed x10, local copies, waits for them, and re-layouts  6.29 us

profile of v2, /device:TPU:10, one launch (start us, length us, event | category | flops | bytes accessed | tf_op | source)
XLA Modules:
  0.0 131.7 jit_solution(10975341300581703188)
XLA Ops:
  0.6 0.7 copy.12
  1.4 0.1 reduce-window.8
  1.4 0.1 reduce
  1.6 0.1 convert_reduce_fusion
  1.6 0.6 broadcast_in_dim.2.job_ref
  2.2 123.2 %shard_map.93 = (bf16[384,1024]{1,0:T(8,128)(2,1)}, bf16[384,2048]{1,0:T(8,128)(2,1)}, f32[256,2048]{1,0:T(8,128)}, f32[256,1024]{1,0:T(8,128)}) custom-call(s32[1,384]{1,0:T(1,128)} %broadcast_in_dim.2.job_ref, bf16[384,2048]{1,0:T(8,128)(2,1)} %hidden_ref.1, bf16[512,2048]{1,0:T(8,128)(2,1)} %bitcast.5, bf16[512,1024]{1,0:T(8,128)(2,1)} %bitcast.7, ...), custom_call_target="tpu_custom_call" | custom-call | tf_op jit(solution)/shard_map/pallas_call | solution.py:529
  125.4 0.0 copy-start.1
  125.4 0.0 copy-start
  125.4 2.2 %copy.17 = bf16[384,1024]{1,0:T(8,128)(2,1)} copy(bf16[384,1024]{1,0:T(8,128)(2,1)} %get-tuple-element.16) | data formatting | bytes 1572864
  127.6 0.0 copy-done.1
  127.6 1.1 copy.18
  128.8 0.0 copy-done
  128.8 0.0 copy-start.2
  128.8 1.3 %copy.19 = f32[16,16,2048]{2,1,0:T(8,128)} copy(f32[16,16,2048]{2,1,0:T(8,128)S(1)} %bitcast.6) | data formatting | bytes 4194304
  130.1 0.6 copy-done.2
  130.7 1.0 copy.20
  (1 shorter events, 0.0 us)
Async XLA Ops:
  125.4 2.2 %copy-start.1 = (bf16[384,2048]{1,0:T(8,128)(2,1)S(1)}, bf16[384,2048]{1,0:T(8,128)(2,1)}, u32[]{:S(2)}) copy-start(bf16[384,2048]{1,0:T(8,128)(2,1)} %get-tuple-element.17) | copy-start | bytes 4718596
  125.4 3.4 %copy-start = (f32[256,2048]{1,0:T(8,128)S(1)}, f32[256,2048]{1,0:T(8,128)}, u32[]{:S(2)}) copy-start(f32[256,2048]{1,0:T(8,128)} %get-tuple-element.10) | copy-start | bytes 6291460
  128.8 2.0 %copy-start.2 = (f32[256,1024]{1,0:T(8,128)S(1)}, f32[256,1024]{1,0:T(8,128)}, u32[]{:S(2)}) copy-start(f32[256,1024]{1,0:T(8,128)} %get-tuple-element.11) | copy-start | bytes 3145732
